TPU v7x, 512 devices: a whole 4x8x8 slice. The times are simulated.
512 devices in a mesh: rows: 32 (over z, x), res: 16 (over y, core).
Axes of the slice: x: 4, y: 8, z: 8, core: 2. Of those that a mesh axis runs over, the one named last changes fastest.
Arguments:
- source_alignment_rows: bfloat16 [2048, 256, 256], P('rows', 'res'), may hold values from -120 to 120
- pairs: int32 [6, 2048], P(None, 'rows'), may hold values from -1 to 2047, as said below
- chain_first_residue: int32 [6], replicated, may hold values from 0 to 235, as said below
- gap_embedding: bfloat16 [256], replicated, may hold values from -4 to 4
- layer_norm_gain: bfloat16 [256], replicated, may hold values from 0.099609375 to 1.8984375
- layer_norm_bias: bfloat16 [256], replicated, may hold values from -3 to 3
- projection_weight: bfloat16 [256, 8, 128], replicated, may hold values from -0.375 to 0.375
- gate_bias_heads: bfloat16 [256], replicated, may hold values from -4 to 4
- pair_bias_logits: bfloat16 [8, 256, 256], P(None, 'res'), may hold values from -6 to 320
- output_weight: bfloat16 [256, 256], replicated, may hold values from -0.375 to 0.375
- output_bias: bfloat16 [256], replicated, may hold values from -3 to 3
Outputs:
- update: bfloat16 [2048, 256, 256], P('rows', 'res')
Inputs may be any that keep to these rules, and one draw needn't show every extreme that they name: `pairs`: within one chain each source row is named at most once; chain 0 has no gaps. For each chain and each aligned block of 64 joint rows, at most 2 entries name rows of one aligned block of 64 source rows, and exactly 2 in some block. chain_first_residue[0] is 0, the starts rise, chain k holds residues from its start up to the next start (the last up to 256), and each chain has at least 21 residues; the last chain has exactly that many.
All inputs are finite; a program needn't handle non-finite values.
Results may differ from a plain program's by a relative error of at most 0.012.
Values may be sent and summed in bfloat16 or wider, within the bound.
A program may use at most 64 MiB of HBM per device.

v0:
```python
import jax
import jax.numpy as jnp
from jax import lax
from jax.sharding import PartitionSpec as P

norm_eps = 1e-05


def layer_norm(values, gain, shift):
    widened = values.astype(jnp.float32)
    center = jnp.mean(widened, axis=-1, keepdims=True)
    spread = jnp.mean(jnp.square(widened - center), axis=-1, keepdims=True)
    scaled = (widened - center) * lax.rsqrt(spread + norm_eps)
    return (scaled * gain.astype(jnp.float32) + shift.astype(jnp.float32)).astype(jnp.bfloat16)


def slot_table(row_lists, owner_ids, block_rows, capacity):
    owner_of = jnp.floor_divide(row_lists, block_rows)
    within = row_lists - owner_of * block_rows
    matches = (row_lists[..., None] >= 0) & (owner_of[..., None] == owner_ids)
    rank_of = jnp.cumsum(matches.astype(jnp.int32), axis=2) - 1
    slot_hit = matches[..., None] & (rank_of[..., None] == jnp.arange(capacity, dtype=jnp.int32))
    slot_list = jnp.sum(slot_hit.astype(jnp.int32) * (within + 1)[..., None, None], axis=2) - 1
    return (slot_list, owner_of, jnp.sum(jnp.where(matches, rank_of, 0), axis=-1))


def attend_core(queries, key_rows, value_rows, gate_rows, bias_rows):
    scores = jnp.einsum("...qd,...kd->...qk", queries, key_rows, preferred_element_type=jnp.float32)
    scores = scores + bias_rows.astype(jnp.float32)
    highest = jnp.max(scores, axis=-1, keepdims=True)
    lifted = jnp.exp(scores - highest)
    weights = (lifted / jnp.sum(lifted, axis=-1, keepdims=True)).astype(jnp.bfloat16)
    summed = jnp.einsum(
        "...qk,...kd->...qd", weights, value_rows, preferred_element_type=jnp.float32
    )
    return (summed * gate_rows.astype(jnp.float32)).astype(jnp.bfloat16)


def local(
    source_alignment_rows,
    pairs,
    chain_first_residue,
    gap_embedding,
    layer_norm_gain,
    layer_norm_bias,
    projection_weight,
    gate_bias_heads,
    pair_bias_logits,
    output_weight,
    output_bias,
):
    local_rows, local_columns, channel_count = source_alignment_rows.shape
    chains = pairs.shape[0]
    owners = lax.axis_size("rows")
    capacity = local_rows // owners
    column_indices = lax.axis_index("res") * local_columns + jnp.arange(
        local_columns, dtype=jnp.int32
    )
    chain_index = jnp.sum(
        (column_indices[:, None] >= chain_first_residue[None, 1:]).astype(jnp.int32), axis=1
    )
    chain_hot = (chain_index[:, None] == jnp.arange(chains, dtype=jnp.int32)[None, :]).astype(
        jnp.int32
    )
    owner_ids = jnp.arange(owners, dtype=jnp.int32)
    requested, owner_of, rank_of = slot_table(pairs[:, None, :], owner_ids, local_rows, capacity)
    wanted = lax.all_to_all(
        jnp.transpose(requested[:, 0], (1, 0, 2)), "rows", split_axis=0, concat_axis=0, tiled=True
    )
    take_rows = jnp.transpose(
        jnp.sum(wanted[:, None, :, :] * chain_hot[None, :, :, None], axis=2), (0, 2, 1)
    )
    col_grid = jnp.arange(local_columns, dtype=jnp.int32)
    flattened_source = source_alignment_rows.reshape(local_rows * local_columns, channel_count)
    outgoing = flattened_source[jnp.maximum(take_rows, 0) * local_columns + col_grid]
    arrived = lax.all_to_all(outgoing, "rows", split_axis=0, concat_axis=0, tiled=True)
    hot_cols = chain_hot.T[:, None, :]
    source_owner = jnp.sum(owner_of[:, 0, :, None] * hot_cols, axis=0)
    source_rank = jnp.sum(rank_of[:, 0, :, None] * hot_cols, axis=0)
    source_list = jnp.sum(pairs[:, :, None] * hot_cols, axis=0)
    arrived_flat = arrived.reshape(owners * capacity * local_columns, channel_count)
    where_from = (jnp.maximum(source_owner, 0) * capacity + source_rank) * local_columns + col_grid[
        None, :
    ]
    joint_rows = jnp.where(
        (source_list >= 0)[..., None], arrived_flat[where_from], gap_embedding[None, None, :]
    )
    normed = layer_norm(joint_rows, layer_norm_gain, layer_norm_bias)
    head_total = projection_weight.shape[1]
    head_dim = projection_weight.shape[2] // 4
    query_scale = head_dim ** (-0.5)
    gate_shift = gate_bias_heads.astype(jnp.float32).reshape(head_total, head_dim)
    out_weight = output_weight.reshape(head_total, head_dim, channel_count)
    full_rows = lax.all_to_all(normed, "res", split_axis=0, concat_axis=1, tiled=True)
    projected = jnp.einsum(
        "rcm,mhe->rhce", full_rows, projection_weight, preferred_element_type=jnp.float32
    )
    queries = (projected[..., :head_dim] * query_scale).astype(jnp.bfloat16)
    key_rows = projected[..., head_dim : 2 * head_dim].astype(jnp.bfloat16)
    value_rows = projected[..., 2 * head_dim : 3 * head_dim].astype(jnp.bfloat16)
    gate_rows = jax.nn.sigmoid(
        projected[..., 3 * head_dim :] + gate_shift[None, :, None, :]
    ).astype(jnp.bfloat16)
    attended = attend_core(
        queries,
        key_rows,
        value_rows,
        gate_rows,
        lax.all_gather(pair_bias_logits, "res", axis=1, tiled=True)[None],
    )
    update = jnp.einsum("rhqd,hdm->rqm", attended, out_weight, preferred_element_type=jnp.float32)
    update = (update + output_bias.astype(jnp.float32)).astype(jnp.bfloat16)
    result = lax.all_to_all(update, "res", split_axis=1, concat_axis=0, tiled=True)
    return result


def solution(mesh):
    return jax.shard_map(
        local,
        mesh=mesh,
        in_specs=(
            P("rows", "res", None),
            P(None, "rows"),
            P(),
            P(),
            P(),
            P(),
            P(),
            P(),
            P(None, "res", None),
            P(),
            P(),
        ),
        out_specs=P("rows", "res", None),
        check_vma=False,
    )
```

profile of v0, /device:TPU:1, one launch (start us, length us, event | category | flops | bytes accessed | tf_op | source)
XLA Modules:
  0.0 140.1 jit_solution(7725693104930153495)
XLA Ops:
  6.5 0.8 add_select_fusion
  7.3 0.7 broadcast_compare_fusion.1
  9.1 0.7 copy.30
  9.9 13.7 %all-to-all-start = ((s32[32,6,2]{1,2,0:T(2,128)}), s32[32,6,2]{1,2,0:T(2,128)S(1)}, u32[]{:S(2)}, u32[]{:S(2)}) async-start(s32[32,6,2]{1,2,0:T(2,128)} %copy.30), calls=%async_computation | async-start | bytes 65536 | tf_op jit(solution)/shard_map/all_to_all | solution.py:67
  23.6 0.7 slice.17
  24.4 7.9 %all-to-all-done = s32[32,6,2]{1,2,0:T(2,128)S(1)} async-done(((s32[32,6,2]{1,2,0:T(2,128)}), s32[32,6,2]{1,2,0:T(2,128)S(1)}, u32[]{:S(2)}, u32[]{:S(2)}) %all-to-all-start) | async-done | bytes 1568 | tf_op jit(solution)/shard_map/all_to_all | solution.py:67
  32.7 5.0 %gather_fusion = bf16[1024,256]{1,0:T(8,128)(2,1)} fusion(bf16[1024,256]{1,0:T(8,128)(2,1)S(1)} %bitcast.50, s32[1024]{0:T(1024)S(1)} %broadcast_clamp_fusion.1), kind=kCustom, calls=%fused_computation | custom fusion | bytes 1052672 | tf_op jit(solution)/shard_map/gather | solution.py:75
  37.7 4.0 %all-to-all-start.1 = ((bf16[32,2,16,256]{3,2,1,0:T(8,128)(2,1)}), bf16[32,2,16,256]{3,2,1,0:T(8,128)(2,1)S(1)}, u32[]{:S(2)}, u32[]{:S(2)}) async-start(bf16[32,2,16,256]{3,2,1,0:T(8,128)(2,1)} %bitcast.4), calls=%async_computation.1 | async-start | bytes 1048576 | tf_op jit(solution)/shard_map/all_to_all | solution.py:76
  41.7 0.7 all-gather.2.cloned.1.call-update
  42.9 13.4 %all-to-all-done.1 = bf16[32,2,16,256]{3,2,1,0:T(8,128)(2,1)S(1)} async-done(((bf16[32,2,16,256]{3,2,1,0:T(8,128)(2,1)}), bf16[32,2,16,256]{3,2,1,0:T(8,128)(2,1)S(1)}, u32[]{:S(2)}, u32[]{:S(2)}) %all-to-all-start.1) | async-done | bytes 524320 | tf_op jit(solution)/shard_map/all_to_all | solution.py:76
  56.4 3.9 %gather_fusion.1 = bf16[1024,256]{1,0:T(8,128)(2,1)S(1)} fusion(bf16[1024,256]{1,0:T(8,128)(2,1)S(1)} %bitcast.51, s32[1024]{0:T(1024)S(1)} %broadcast_clamp_fusion), kind=kCustom, calls=%fused_computation.1 | custom fusion | bytes 1052672 | tf_op jit(solution)/shard_map/gather | solution.py:86
  60.3 0.4 convert_reduce_fusion
  60.7 0.5 fusion.12
  61.2 1.3 fusion.15
  62.5 11.7 %all-to-all-start.2 = ((bf16[64,16,256]{2,1,0:T(8,128)(2,1)}), bf16[64,16,256]{2,1,0:T(8,128)(2,1)}, u32[]{:S(2)}, u32[]{:S(2)}) async-start(bf16[64,16,256]{2,1,0:T(8,128)(2,1)} %fusion.15), calls=%async_computation.2 | async-start | bytes 1048576 | tf_op jit(solution)/shard_map/all_to_all | solution.py:94
  74.6 17.3 %all-gather.2.cloned.1.call-done = bf16[8,256,256]{2,1,0:T(8,128)(2,1)} async-done(((bf16[8,16,256]{2,1,0:T(8,128)(2,1)}), bf16[8,256,256]{2,1,0:T(8,128)(2,1)}) %all-gather.2.cloned.1.call-update) | async-done | bytes 1048592 | tf_op jit(solution)/shard_map/all_gather | solution.py:109
  91.9 1.5 %copy.36 = f32[8,256,256]{1,2,0:T(8,128)S(1)} copy(bf16[8,256,256]{2,1,0:T(8,128)(2,1)} %all-gather.2.cloned.1.call-done) | data formatting | bytes 3145728 | tf_op jit(solution)/shard_map/convert_element_type | solution.py:29
  93.4 1.1 copy.34
  94.4 3.5 %fusion.54 = (bf16[4,8,256,128]{2,3,1,0:T(8,128)(2,1)}, f32[4,8,256,128]{2,3,1,0:T(8,128)}) fusion(bf16[4,256,256,1]{2,1,3,0:T(8,128)(2,1)S(1)} %bitcast.54, bf16[256,8,128]{0,2,1:T(8,128)(2,1)S(1)} %copy.35), kind=kOutput, calls=%fused_computation.82 | convolution fusion | flops 537919488 | bytes 7340032 | tf_op jit(solution)/shard_map/rcm,mhe->rhce/dot_general | solution.py:95
  97.9 7.3 %fusion.55 = (f32[4,8,256]{2,1,0:T(8,128)S(1)}, f32[4,8,256,256]{2,3,1,0:T(8,128)}) fusion(f32[8,256,256]{1,2,0:T(8,128)S(1)} %copy.36, bf16[4,8,256,128]{2,3,1,0:T(8,128)(2,1)} %get-tuple-element.12, f32[4,8,256,128]{2,3,1,0:T(8,128)} %get-tuple-element.13), kind=kOutput, calls=%fused_computation.83 | convolution fusion | flops 141033728 | bytes 12091392 | tf_op jit(solution)/shard_map/sub | solution.py:31
  105.2 5.0 %fusion.9 = bf16[4,256,256]{2,1,0:T(8,128)(2,1)S(1)} fusion(bf16[8,32,256,1]{2,1,0,3:T(8,128)(2,1)S(1)} %bitcast.56, f32[4,8,256,256]{2,3,1,0:T(8,128)} %get-tuple-element.15, f32[4,8,256]{2,1,0:T(8,128)S(1)} %get-tuple-element.14, f32[4,8,256,128]{2,3,1,0:T(8,128)} %get-tuple-element.13, bf16[4,8,256,128]{2,3,1,0:T(8,128)(2,1)} %get-tuple-element.12, ...), kind=kOutput, calls=%fused_computation.16 | convolution fusion | flops 275251200 | bytes 10651648 | tf_op jit(solution)/shard_map/rhqd,hdm->rqm/dot_general | solution.py:111
  110.2 0.4 copy.38
  110.6 21.8 %all_to_all.46 = bf16[4,256,256]{2,0,1:T(4,128)(2,1)S(1)} all-to-all(bf16[4,256,256]{2,0,1:T(4,128)(2,1)S(1)} %copy.38), channel_id=1, replica_groups=mesh['rows'=32,'res'=16] {'res'}, dimensions={1} | all-to-all | bytes 1048576 | tf_op jit(solution)/shard_map/all_to_all | solution.py:113
  132.4 0.9 copy.39
  (51 shorter events, 2.5 us)
Async XLA Ops:
  6.5 26.1 %copy-start = (bf16[64,16,256]{2,1,0:T(8,128)(2,1)S(1)}, bf16[64,16,256]{2,1,0:T(8,128)(2,1)}, u32[]{:S(2)}) copy-start(bf16[64,16,256]{2,1,0:T(8,128)(2,1)} %param.11) | copy-start | bytes 1572868
  6.5 35.9 %copy-start.2 = (s32[6,64]{1,0:T(8,128)S(1)}, s32[6,64]{1,0:T(8,128)}, u32[]{:S(2)}) copy-start(s32[6,64]{1,0:T(8,128)} %param.12) | copy-start | bytes 4612
  6.5 36.3 %copy-start.6 = (bf16[256]{0:T(256)(128)(2,1)S(1)}, bf16[256]{0:T(256)(128)(2,1)}, u32[]{:S(2)}) copy-start(bf16[256]{0:T(256)(128)(2,1)} %param.15) | copy-start | bytes 1540
  6.5 36.3 %copy-start.7 = (bf16[256]{0:T(256)(128)(2,1)S(1)}, bf16[256]{0:T(256)(128)(2,1)}, u32[]{:S(2)}) copy-start(bf16[256]{0:T(256)(128)(2,1)} %param.16) | copy-start | bytes 1540
  9.9 22.4 %all-to-all-start = ((s32[32,6,2]{1,2,0:T(2,128)}), s32[32,6,2]{1,2,0:T(2,128)S(1)}, u32[]{:S(2)}, u32[]{:S(2)}) async-start(s32[32,6,2]{1,2,0:T(2,128)} %copy.30), calls=%async_computation | async-start | bytes 65536 | tf_op jit(solution)/shard_map/all_to_all | solution.py:67
  37.7 22.6 %copy-start.3 = (bf16[256]{0:T(256)(128)(2,1)S(1)}, bf16[256]{0:T(256)(128)(2,1)}, u32[]{:S(2)}) copy-start(bf16[256]{0:T(256)(128)(2,1)} %param.14) | copy-start | bytes 1540
  37.7 18.7 %all-to-all-start.1 = ((bf16[32,2,16,256]{3,2,1,0:T(8,128)(2,1)}), bf16[32,2,16,256]{3,2,1,0:T(8,128)(2,1)S(1)}, u32[]{:S(2)}, u32[]{:S(2)}) async-start(bf16[32,2,16,256]{3,2,1,0:T(8,128)(2,1)} %bitcast.4), calls=%async_computation.1 | async-start | bytes 1048576 | tf_op jit(solution)/shard_map/all_to_all | solution.py:76
  41.7 50.2 %all-gather.2.cloned.1.call-start = ((), (), s32[]{:S(2)}) async-start(), calls=%async_computation.4 | async-start | bytes 1114112 | tf_op jit(solution)/shard_map/all_gather | solution.py:109
  42.5 31.7 %copy-start.1 = (bf16[256,8,128]{2,1,0:T(8,128)(2,1)S(1)}, bf16[256,8,128]{2,1,0:T(8,128)(2,1)}, u32[]{:S(2)}) copy-start(bf16[256,8,128]{2,1,0:T(8,128)(2,1)} %param.17) | copy-start | bytes 1572868
  56.3 18.1 %copy-start.4 = (bf16[256]{0:T(256)(128)(2,1)S(1)}, bf16[256]{0:T(256)(128)(2,1)}, u32[]{:S(2)}) copy-start(bf16[256]{0:T(256)(128)(2,1)} %param.18) | copy-start | bytes 1540
  56.4 18.2 %copy-start.8 = (bf16[256]{0:T(256)(128)(2,1)S(1)}, bf16[256]{0:T(256)(128)(2,1)}, u32[]{:S(2)}) copy-start(bf16[256]{0:T(256)(128)(2,1)} %param.21) | copy-start | bytes 1540
  62.5 30.9 %all-to-all-start.2 = ((bf16[64,16,256]{2,1,0:T(8,128)(2,1)}), bf16[64,16,256]{2,1,0:T(8,128)(2,1)}, u32[]{:S(2)}, u32[]{:S(2)}) async-start(bf16[64,16,256]{2,1,0:T(8,128)(2,1)} %fusion.15), calls=%async_computation.2 | async-start | bytes 1048576 | tf_op jit(solution)/shard_map/all_to_all | solution.py:94
  97.9 7.3 %copy-start.5 = (bf16[256,256]{1,0:T(8,128)(2,1)S(1)}, bf16[256,256]{1,0:T(8,128)(2,1)}, u32[]{:S(2)}) copy-start(bf16[256,256]{1,0:T(8,128)(2,1)} %param.20) | copy-start | bytes 393220
Sparse Core Ops, SparseCore 0:
  44.7 47.1 all-gather.1
where the time goes:
time: 141 us; the launch traced here: 140 us
  waiting for transfers between devices  39.3 us (28%)
  starting transfers between devices  29.4 us (21%)
  blocking collectives  21.8 us (15%)
  matrix products  15.7 us (11%)
  local copies, waits for them, and re-layouts  15.3 us (11%)
  between operations  13.7 us (10%)
  other arithmetic  4.95 us (4%)
    all_to_all x1, blocking collectives, local(): lax.all_to_all(update, 'res', split_axis=1, concat_axis=0, tiled=True)  21.8 us
    all_gather x1, waiting for transfers between devices, local(): lax.all_gather(pair_bias_logits, 'res', axis=1, tiled=True)[None]  17.3 us
    all_to_all x1, starting transfers between devices, local(): lax.all_to_all(jnp.transpose(requested[:, 0], (1, 0, 2)), 'rows', split_a...  13.7 us
    all_to_all x1, waiting for transfers between devices, local(): lax.all_to_all(outgoing, 'rows', split_axis=0, concat_axis=0, tiled=True)  13.4 us
    all_to_all x1, starting transfers between devices, local(): lax.all_to_all(normed, 'res', split_axis=0, concat_axis=1, tiled=True)  11.7 us
    all_to_all x1, waiting for transfers between devices, local(): lax.all_to_all(jnp.transpose(requested[:, 0], (1, 0, 2)), 'rows', split_a...  7.86 us
    sub x1, matrix products, attend_core(): lifted = jnp.exp(scores - highest)  7.29 us
    gather x1, local copies, waits for them, and re-layouts, local(): flattened_source[jnp.maximum(take_rows, 0) * local_columns + col_grid]  4.98 us
  transfers between devices with their start and end apart: 4, of which 3 were waited for; matrix products, arithmetic and copies ran while one was open for 7% of the time, Pallas kernels for 0%

commit v1 on v0

v1 whole, which is shorter than its diff:
```python
import functools
import math

import jax
import jax.numpy as jnp
from jax import lax
from jax.experimental import pallas as pl
from jax.experimental.pallas import tpu as pltpu
from jax.sharding import PartitionSpec as P

norm_eps = 1e-05
MESH = pl.DeviceIdType.MESH
f32, bf16, i32 = jnp.float32, jnp.bfloat16, jnp.int32
NT = (((1,), (1,)), ((), ()))
TN = (((0,), (0,)), ((), ()))
CHAIN_PAD = 8


def layer_norm(x, gain, shift):
    center = jnp.mean(x, axis=-1, keepdims=True)
    moved = x - center
    spread = jnp.mean(jnp.square(moved), axis=-1, keepdims=True)
    return moved * lax.rsqrt(spread + norm_eps) * gain + shift


def body(
    R, J, n, cols, heads, chains,
    first_ref, pairs_ref, vec_ref, src_hbm, w_hbm, bias_hbm, ow_hbm,
    out_hbm,
    src_v, norm_v, w_v, w_wide, wqvg_t, wk_t, ow_v,
    table_v, wanted_v, wanted_s, pos_v, pos_s,
    bias_all, bias_t,
    send_a0, send_a1, recv_a0, recv_a1,
    send_b0, send_b1, recv_b0, recv_b1,
    q_diag, att_v, send_c, gate_col,
    local_sem, idx_send, idx_recv, bias_send, bias_recv,
    a_send, a_recv, b_send, b0_recv, b1_recv, c_send, c_recv,
):
    L = n * J
    width = 256
    half = width // 2
    N = J * cols
    hd = width // heads
    Y = J // 2
    log2e = math.log2(math.e)
    me_r = lax.axis_index("rows")
    me_j = lax.axis_index("res")
    core = lax.rem(me_j, 2)

    def row_peer(t):
        return lax.rem(me_r + t, R)

    def res_peer(t):
        return lax.rem(me_j + t, J)

    load_src = pltpu.make_async_copy(src_hbm, src_v, local_sem.at[0])
    load_w = pltpu.make_async_copy(w_hbm, w_v, local_sem.at[1])
    load_bias = pltpu.make_async_copy(
        bias_hbm, bias_all.at[me_j // 2, core], local_sem.at[2]
    )
    load_ow = pltpu.make_async_copy(ow_hbm, ow_v, local_sem.at[3])
    load_src.start()
    load_bias.start()
    load_w.start()
    load_ow.start()

    barrier = pltpu.get_barrier_semaphore()

    @pl.loop(1, R)
    def _(t):
        pl.semaphore_signal(
            barrier, inc=1, device_id={"rows": row_peer(t)}, device_id_type=MESH
        )

    @pl.loop(1, J)
    def _(t):
        pl.semaphore_signal(
            barrier, inc=1, device_id={"res": res_peer(t)}, device_id_type=MESH
        )

    listed = pairs_ref[...]
    shift_bits = L.bit_length() - 1
    owner = lax.shift_right_arithmetic(listed, jnp.full_like(listed, shift_bits))
    within = jnp.bitwise_and(listed, L - 1)
    lane = lax.broadcasted_iota(i32, (R, 128), 1)
    row_id = lax.broadcasted_iota(i32, (R, L), 0)
    table = jnp.zeros((R, 128), i32)
    for c in range(chains):
        own_c = owner[c : c + 1, :]
        wit_c = within[c : c + 1, :]
        match = row_id == own_c
        low = jnp.min(jnp.where(match, wit_c, L), axis=1, keepdims=True)
        high = jnp.max(jnp.where(match, wit_c, -1), axis=1, keepdims=True)
        table = jnp.where(lane == c, jnp.minimum(low, L - 1), table)
        table = jnp.where(lane == CHAIN_PAD + c, jnp.maximum(high, 0), table)
        rank = jnp.max(
            jnp.where(match, jnp.where(wit_c > low, 1, 0), 0), axis=0, keepdims=True
        )
        pos_v[c : c + 1, 0:L] = jnp.where(own_c < 0, 2 * R, 2 * own_c + rank)
    table_v[...] = table.reshape(R, 1, 128)
    load_pos = pltpu.make_async_copy(pos_v, pos_s, local_sem.at[4])
    load_pos.start()

    col0 = me_j * cols
    chain_a = jnp.int32(0)
    chain_b = jnp.int32(0)
    for k in range(1, chains):
        chain_a += (first_ref[k] <= col0).astype(i32)
        chain_b += (first_ref[k] <= col0 + cols - 1).astype(i32)
    start_b = first_ref[chain_b] - col0
    in_b = lax.broadcasted_iota(i32, (cols, width), 0) >= start_b
    in_b_half = lax.broadcasted_iota(i32, (cols, half), 0) >= start_b

    pl.semaphore_wait(barrier, R - 1 + J - 1)

    wanted_v[me_r] = table_v[me_r]

    @pl.loop(1, R)
    def _(t):
        b = row_peer(t)
        pltpu.make_async_remote_copy(
            table_v.at[b], wanted_v.at[me_r], idx_send, idx_recv,
            device_id={"rows": b}, device_id_type=MESH,
        ).start()

    load_bias.wait()
    my_bias = bias_all.at[me_j // 2, core]

    @pl.loop(1, Y)
    def _(t):
        pltpu.make_async_remote_copy(
            my_bias, my_bias, bias_send.at[0], bias_recv.at[0],
            device_id={"res": res_peer(2 * t)}, device_id_type=MESH,
        ).start()

    gap = vec_ref[0:1, :]
    gain = vec_ref[1:2, :]
    shift = vec_ref[2:3, :]
    out_shift = vec_ref[3:4, :]
    load_src.wait()
    step = 4

    @pl.loop(0, L // step)
    def _(i):
        x = src_v[pl.ds(i * step, step)].astype(f32).reshape(step * cols, width)
        y = layer_norm(x, gain, shift).astype(bf16)
        norm_v[pl.ds(i * step, step)] = y.reshape(step, cols, width)

    gap_row = jnp.broadcast_to(layer_norm(gap, gain, shift), (cols, width)).astype(bf16)
    recv_a0[2 * R] = gap_row[:, :half]
    recv_a1[2 * R] = gap_row[:, half:]

    def wait_recv(ref, sem):
        pltpu.make_async_remote_copy(
            ref, ref, idx_send, sem, device_id={"rows": me_r}, device_id_type=MESH
        ).wait_recv()

    def wait_send(ref, sem):
        pltpu.make_async_remote_copy(
            ref, ref, sem, idx_recv, device_id={"rows": me_r}, device_id_type=MESH
        ).wait_send()

    wait_recv(wanted_v.at[pl.ds(0, R - 1)], idx_recv)
    load_wanted = pltpu.make_async_copy(wanted_v, wanted_s, local_sem.at[5])
    load_wanted.start()
    load_wanted.wait()
    load_pos.wait()

    def pick(b, k):
        at_a = jnp.clip(wanted_s[b, 0, k * CHAIN_PAD + chain_a], 0, L - 1)
        at_b = jnp.clip(wanted_s[b, 0, k * CHAIN_PAD + chain_b], 0, L - 1)
        return jnp.where(in_b, norm_v[at_b], norm_v[at_a])

    @pl.loop(1, R)
    def _(t):
        b = row_peer(t)
        for k in range(2):
            cells = pick(b, k)
            send_a0[b, k] = cells[:, :half]
            send_a1[b, k] = cells[:, half:]
        pltpu.make_async_remote_copy(
            send_a0.at[b], recv_a0.at[pl.ds(2 * me_r, 2)], a_send.at[0], a_recv.at[0],
            device_id={"rows": b}, device_id_type=MESH,
        ).start()

    @pl.loop(1, R)
    def _(t):
        b = row_peer(t)
        pltpu.make_async_remote_copy(
            send_a1.at[b], recv_a1.at[pl.ds(2 * me_r, 2)], a_send.at[1], a_recv.at[1],
            device_id={"rows": b}, device_id_type=MESH,
        ).start()

    for k in range(2):
        cells = pick(me_r, k)
        recv_a0[2 * me_r + k] = cells[:, :half]
        recv_a1[2 * me_r + k] = cells[:, half:]

    load_w.wait()
    load_ow.wait()
    w_wide[...] = w_v[...].astype(f32).reshape(width * heads, 128)
    q_diag[...] = jnp.zeros_like(q_diag)
    for h in range(heads):
        w_h = w_wide[pl.ds(h, width, stride=heads), :].T.astype(bf16)
        own = slice(h * hd, (h + 1) * hd)
        wqvg_t[0 * width + h * hd : 0 * width + (h + 1) * hd, :] = w_h[0:hd]
        wk_t[own, :] = w_h[hd : 2 * hd]
        wqvg_t[1 * width + h * hd : 1 * width + (h + 1) * hd, :] = w_h[2 * hd : 3 * hd]
        wqvg_t[2 * width + h * hd : 2 * width + (h + 1) * hd, :] = w_h[3 * hd :]
    gate_col[...] = jnp.broadcast_to(vec_ref[4:5, :], (128, width)).T

    wait_recv(recv_a0.at[pl.ds(0, 2 * (R - 1))], a_recv.at[0])

    def regather(recv, s):
        at_a = jnp.clip(pos_s[chain_a, s], 0, 2 * R)
        at_b = jnp.clip(pos_s[chain_b, s], 0, 2 * R)
        return jnp.where(in_b_half, recv[at_b], recv[at_a])

    @pl.loop(1, J)
    def _(t):
        j = res_peer(t)
        for r in range(n):
            send_b0[j, r] = regather(recv_a0, j * n + r)
        pltpu.make_async_remote_copy(
            send_b0.at[j], recv_b0.at[:, me_j], b_send.at[0], b0_recv,
            device_id={"res": j}, device_id_type=MESH,
        ).start()

    for r in range(n):
        recv_b0[r, me_j] = regather(recv_a0, me_j * n + r)

    wait_recv(bias_all.at[pl.ds(0, Y - 1), 0], bias_recv.at[0])
    share = bias_all.at[:, core]
    pltpu.make_async_remote_copy(
        share, share, bias_send.at[1], bias_recv.at[1],
        device_id={"res": me_j + 1 - 2 * core}, device_id_type=MESH,
    ).start()

    wait_recv(recv_a1.at[pl.ds(0, 2 * (R - 1))], a_recv.at[1])

    @pl.loop(0, n)
    def _(r):
        @pl.loop(1, J)
        def _(t):
            j = res_peer(t)
            send_b1[r, j] = regather(recv_a1, j * n + r)
            pltpu.make_async_remote_copy(
                send_b1.at[r, j], recv_b1.at[r, me_j], b_send.at[1], b1_recv.at[r],
                device_id={"res": j}, device_id_type=MESH,
            ).start()

        recv_b1[r, me_j] = regather(recv_a1, me_j * n + r)

    wait_recv(bias_all.at[:, 0], bias_recv.at[1])
    for h in range(heads):
        block = bias_all[:, :, h].reshape(N, N).astype(f32)
        bias_t[h] = block.T * log2e

    wait_recv(recv_b0.at[:, pl.ds(0, J - 1)], b0_recv)
    scale = hd ** (-0.5) * log2e

    @pl.loop(0, n)
    def _(r):
        wait_recv(recv_b1.at[r, pl.ds(0, J - 1)], b1_recv.at[r])
        x = jnp.concatenate(
            [recv_b0[r].reshape(N, half), recv_b1[r].reshape(N, half)], axis=1
        )
        qvg = lax.dot_general(wqvg_t[...], x, NT, preferred_element_type=f32)
        keys = lax.dot_general(x, wk_t[...], NT, preferred_element_type=f32).astype(bf16)
        q = (qvg[:width] * scale).astype(bf16)
        v = qvg[width : 2 * width].astype(bf16)
        gate = jax.nn.sigmoid(qvg[2 * width :] + gate_col[:, 0:1])
        ones = jnp.ones((16, N), bf16)
        for h in range(heads):
            own = slice(h * hd, (h + 1) * hd)
            q_diag[h, own, :] = q[own]
            s = jnp.dot(keys, q_diag[h], preferred_element_type=f32) + bias_t[h]
            top = jnp.max(s, axis=0, keepdims=True)
            e = jnp.exp2(s - top).astype(bf16)
            o = jnp.dot(
                jnp.concatenate([v[own], ones], axis=0), e, preferred_element_type=f32
            )
            att_v[own, :] = (o[:hd] * (1.0 / o[hd : hd + 1]) * gate[own]).astype(bf16)
        update = lax.dot_general(att_v[...], ow_v[...], TN, preferred_element_type=f32)
        update = (update + out_shift).astype(bf16)
        send_c[pl.ds(r * J, J)] = update.reshape(J, cols, width)

        @pl.loop(1, J)
        def _(t):
            j = res_peer(t)
            pltpu.make_async_remote_copy(
                send_c.at[r * J + j], out_hbm.at[me_j * n + r], c_send, c_recv,
                device_id={"res": j}, device_id_type=MESH,
            ).start()

        pltpu.make_async_copy(
            send_c.at[r * J + me_j], out_hbm.at[me_j * n + r], local_sem.at[6 + r]
        ).start()

    for r in range(n):
        pltpu.make_async_copy(
            send_c.at[r * J + me_j], out_hbm.at[me_j * n + r], local_sem.at[6 + r]
        ).wait()
    wait_send(table_v.at[pl.ds(0, R - 1)], idx_send)
    wait_send(bias_all.at[pl.ds(0, Y - 1), 0], bias_send.at[0])
    wait_send(bias_all.at[:, 0], bias_send.at[1])
    wait_send(send_a0.at[pl.ds(0, R - 1)], a_send.at[0])
    wait_send(send_a1.at[pl.ds(0, R - 1)], a_send.at[1])
    wait_send(send_b0.at[pl.ds(0, J - 1)], b_send.at[0])
    wait_send(send_b1.at[:, pl.ds(0, J - 1)], b_send.at[1])
    wait_send(send_c.at[pl.ds(0, n * (J - 1))], c_send)
    wait_recv(out_hbm.at[pl.ds(0, n * (J - 1))], c_recv)


def local(
    source_alignment_rows,
    pairs,
    chain_first_residue,
    gap_embedding,
    layer_norm_gain,
    layer_norm_bias,
    projection_weight,
    gate_bias_heads,
    pair_bias_logits,
    output_weight,
    output_bias,
):
    R, J = lax.axis_size("rows"), lax.axis_size("res")
    L, cols, width = source_alignment_rows.shape
    heads = projection_weight.shape[1]
    chains = pairs.shape[0]
    n = L // J
    N = J * cols
    half = width // 2
    vectors = jnp.stack(
        [gap_embedding, layer_norm_gain, layer_norm_bias, output_bias, gate_bias_heads]
    ).astype(f32)
    DMA = pltpu.SemaphoreType.DMA
    vmem, anywhere = pl.BlockSpec(memory_space=pltpu.VMEM), pl.BlockSpec(memory_space=pl.ANY)
    return pl.pallas_call(
        functools.partial(body, R, J, n, cols, heads, chains),
        out_shape=jax.ShapeDtypeStruct((L, cols, width), bf16),
        in_specs=[
            pl.BlockSpec(memory_space=pltpu.SMEM), vmem, vmem,
            anywhere, anywhere, anywhere, anywhere,
        ],
        out_specs=anywhere,
        scratch_shapes=[
            pltpu.VMEM((L, cols, width), bf16),
            pltpu.VMEM((L, cols, width), bf16),
            pltpu.VMEM((width, heads, 128), bf16),
            pltpu.VMEM((width * heads, 128), f32),
            pltpu.VMEM((3 * width, width), bf16),
            pltpu.VMEM((width, width), bf16),
            pltpu.VMEM((width, width), bf16),
            pltpu.VMEM((R, 1, 128), i32),
            pltpu.VMEM((R, 1, 128), i32),
            pltpu.SMEM((R, 1, 128), i32),
            pltpu.VMEM((8, 128), i32),
            pltpu.SMEM((8, 128), i32),
            pltpu.VMEM((J // 2, 2, heads, cols, N), bf16),
            pltpu.VMEM((heads, N, N), f32),
            pltpu.VMEM((R, 2, cols, half), bf16),
            pltpu.VMEM((R, 2, cols, half), bf16),
            pltpu.VMEM((2 * R + 1, cols, half), bf16),
            pltpu.VMEM((2 * R + 1, cols, half), bf16),
            pltpu.VMEM((J, n, cols, half), bf16),
            pltpu.VMEM((n, J, cols, half), bf16),
            pltpu.VMEM((n, J, cols, half), bf16),
            pltpu.VMEM((n, J, cols, half), bf16),
            pltpu.VMEM((heads, width, N), bf16),
            pltpu.VMEM((width, N), bf16),
            pltpu.VMEM((n * J, cols, width), bf16),
            pltpu.VMEM((width, 128), f32),
            DMA((6 + n,)), DMA, DMA, DMA((2,)), DMA((2,)),
            DMA((2,)), DMA((2,)), DMA((2,)), DMA, DMA((n,)), DMA, DMA,
        ],
        compiler_params=pltpu.CompilerParams(
            collective_id=0, has_side_effects=True, vmem_limit_bytes=40 * 1024 * 1024
        ),
    )(
        chain_first_residue, pairs, vectors, source_alignment_rows, projection_weight,
        pair_bias_logits, output_weight,
    )


def solution(mesh):
    return jax.shard_map(
        local,
        mesh=mesh,
        in_specs=(
            P("rows", "res", None),
            P(None, "rows"),
            P(),
            P(),
            P(),
            P(),
            P(),
            P(),
            P(None, "res", None),
            P(),
            P(),
        ),
        out_specs=P("rows", "res", None),
        check_vma=False,
    )
```

time: 141 us -> 69.8 us (0.50)
  Pallas kernels: 0 us -> 61.4 us
  waiting for transfers between devices: 39.3 us -> 0 us
  starting transfers between devices: 29.4 us -> 0 us
  blocking collectives: 21.8 us -> 0 us
  matrix products: 15.7 us -> 0 us
  between operations: 13.7 us -> 0.04 us
  local copies, waits for them, and re-layouts: 15.3 us -> 7.95 us
  other arithmetic: 4.95 us -> 0.01 us
    pallas_call x0 -> x1, Pallas kernels: none -> 61.4 us  [local(): pl.pallas_call(functools.partial(body, R, J, n, cols, heads, chains), out...]
    all_to_all x3 -> x0, starting transfers between devices: 29.4 us -> none  [the longest x1 13.7 us: local(): lax.all_to_all(jnp.transpose(requested[:, 0], (1, 0, 2)), 'rows', split_a...]
    all_to_all x1 -> x0, blocking collectives: 21.8 us -> none  [local(): lax.all_to_all(update, 'res', split_axis=1, concat_axis=0, tiled=True)]
    all_to_all x3 -> x0, waiting for transfers between devices: 21.3 us -> none  [the longest x1 13.4 us: local(): lax.all_to_all(outgoing, 'rows', split_axis=0, concat_axis=0, tiled=True)]
    all_gather x1 -> x0, waiting for transfers between devices: 17.3 us -> none  [local(): lax.all_gather(pair_bias_logits, 'res', axis=1, tiled=True)[None]]
    gather x2 -> x0, local copies, waits for them, and re-layouts: 8.92 us -> none  [the longest x1 4.98 us: local(): flattened_source[jnp.maximum(take_rows, 0) * local_columns + col_grid]]
    dot_general x2 -> x0, matrix products: 8.44 us -> none  [the longest x1 4.98 us: local(): jnp.einsum('rhqd,hdm->rqm', attended, out_weight, preferred_element_type=...]
    sub x1 -> x0, matrix products: 7.29 us -> none  [attend_core(): lifted = jnp.exp(scores - highest)]
  transfers between devices with their start and end apart: 4 -> 0, of which waited for: 3 -> 0; matrix products, arithmetic and copies ran while one was open for 7% -> 0% of each run, Pallas kernels for 0% -> 0%
where the time goes in v1:
time: 69.8 us; the launch traced here: 69.4 us
  Pallas kernels  61.4 us (88%)
  local copies, waits for them, and re-layouts  7.95 us (11%)
    pallas_call x1, Pallas kernels, local(): pl.pallas_call(functools.partial(body, R, J, n, cols, heads, chains), out...  61.4 us
    unnamed x21, local copies, waits for them, and re-layouts  7.24 us

profile of v1, /device:TPU:1, one launch (start us, length us, event | category | flops | bytes accessed | tf_op | source)
XLA Modules:
  0.0 69.4 jit_solution(11986304820014902961)
XLA Ops:
  0.0 0.0 copy-start.6
  0.0 0.7 stack.18
  0.7 0.0 copy-done.6
  0.7 0.0 copy-start.7
  0.7 0.6 copy-done.7
  1.3 0.0 copy-start.8
  1.3 0.6 copy-done.8
  2.0 0.0 copy-start.9
  2.0 0.6 copy-done.9
  2.7 0.0 copy-start.4
  2.7 0.0 copy-start.5
  2.7 0.7 copy-done.4
  3.4 0.0 copy-done.5
  3.4 0.0 copy-start
  3.4 1.0 %copy-done = bf16[64,16,256]{2,1,0:T(8,128)(2,1)S(1)} copy-done((bf16[64,16,256]{2,1,0:T(8,128)(2,1)S(1)}, bf16[64,16,256]{2,1,0:T(8,128)(2,1)}, u32[]{:S(2)}) %copy-start) | copy-done | bytes 524312
  4.4 0.0 copy-start.1
  4.4 1.0 %copy-done.1 = bf16[256,8,128]{2,1,0:T(8,128)(2,1)S(1)} copy-done((bf16[256,8,128]{2,1,0:T(8,128)(2,1)S(1)}, bf16[256,8,128]{2,1,0:T(8,128)(2,1)}, u32[]{:S(2)}) %copy-start.1) | copy-done | bytes 524312
  5.5 0.0 copy-start.2
  5.5 0.9 %copy-done.2 = bf16[256,256]{1,0:T(8,128)(2,1)S(1)} copy-done((bf16[256,256]{1,0:T(8,128)(2,1)S(1)}, bf16[256,256]{1,0:T(8,128)(2,1)}, u32[]{:S(2)}) %copy-start.2) | copy-done | bytes 131096
  6.4 0.0 copy-start.3
  6.4 0.8 %copy-done.3 = bf16[8,16,256]{2,1,0:T(8,128)(2,1)S(1)} copy-done((bf16[8,16,256]{2,1,0:T(8,128)(2,1)S(1)}, bf16[8,16,256]{2,1,0:T(8,128)(2,1)}, u32[]{:S(2)}) %copy-start.3) | copy-done | bytes 65560
  7.2 61.4 %shard_map.109 = bf16[64,16,256]{2,1,0:T(8,128)(2,1)S(1)} custom-call(s32[6]{0:T(128)S(1)} %copy-done.5, s32[6,64]{1,0:T(8,128)S(1)} %copy-done.4, f32[5,256]{1,0:T(8,128)S(1)} %convert_element_type.3.vec_ref, bf16[64,16,256]{2,1,0:T(8,128)(2,1)S(1)} %copy-done, bf16[256,8,128]{2,1,0:T(8,128)(2,1)S(1)} %copy-done.1, bf16[8,16,256]{2,1,0:T(8,128)(2,1)S(1)} %copy-done.3, ...), custom_call_target="tpu_custom_call" | custom-call | tf_op jit(solution)/shard_map/pallas_call | solution.py:340
  68.6 0.8 %copy.13 = bf16[64,16,256]{2,1,0:T(8,128)(2,1)} copy(bf16[64,16,256]{2,1,0:T(8,128)(2,1)S(1)} %shard_map.109) | data formatting | bytes 1048576
  (6 shorter events, 0.0 us)
Async XLA Ops:
  0.0 0.7 copy-start.6
  0.7 0.7 copy-start.7
  1.3 0.7 copy-start.8
  2.0 0.7 copy-start.9
  2.7 0.7 copy-start.4
  2.7 0.7 copy-start.5
  3.4 1.0 %copy-start = (bf16[64,16,256]{2,1,0:T(8,128)(2,1)S(1)}, bf16[64,16,256]{2,1,0:T(8,128)(2,1)}, u32[]{:S(2)}) copy-start(bf16[64,16,256]{2,1,0:T(8,128)(2,1)} %src_hbm.1) | copy-start | bytes 1572868
  4.4 1.0 %copy-start.1 = (bf16[256,8,128]{2,1,0:T(8,128)(2,1)S(1)}, bf16[256,8,128]{2,1,0:T(8,128)(2,1)}, u32[]{:S(2)}) copy-start(bf16[256,8,128]{2,1,0:T(8,128)(2,1)} %w_hbm.1) | copy-start | bytes 1572868
  5.5 0.9 %copy-start.2 = (bf16[256,256]{1,0:T(8,128)(2,1)S(1)}, bf16[256,256]{1,0:T(8,128)(2,1)}, u32[]{:S(2)}) copy-start(bf16[256,256]{1,0:T(8,128)(2,1)} %ow_hbm.1) | copy-start | bytes 393220
  6.4 0.8 %copy-start.3 = (bf16[8,16,256]{2,1,0:T(8,128)(2,1)S(1)}, bf16[8,16,256]{2,1,0:T(8,128)(2,1)}, u32[]{:S(2)}) copy-start(bf16[8,16,256]{2,1,0:T(8,128)(2,1)} %bias_hbm.1) | copy-start | bytes 196612

commit v2 on v1

--- a/solution.py
+++ b/solution.py
@@ -25,8 +25,10 @@
 
 def body(
     R, J, n, cols, heads, chains,
-    first_ref, pairs_ref, vec_ref, src_hbm, w_hbm, bias_hbm, ow_hbm,
+    first_hbm, pairs_hbm, gap_hbm, gain_hbm, shift_hbm, out_shift_hbm, gate_hbm,
+    src_hbm, w_hbm, bias_hbm, ow_hbm,
     out_hbm,
+    first_ref, pairs_ref, vec_refs,
     src_v, norm_v, w_v, w_wide, wqvg_t, wk_t, ow_v,
     table_v, wanted_v, wanted_s, pos_v, pos_s,
     bias_all, bias_t,
@@ -59,7 +61,17 @@
         bias_hbm, bias_all.at[me_j // 2, core], local_sem.at[2]
     )
     load_ow = pltpu.make_async_copy(ow_hbm, ow_v, local_sem.at[3])
+    load_first = pltpu.make_async_copy(first_hbm, first_ref, local_sem.at[6])
+    load_pairs = pltpu.make_async_copy(pairs_hbm, pairs_ref, local_sem.at[7])
+    load_vecs = [
+        pltpu.make_async_copy(v, vec_refs[i], local_sem.at[8 + i])
+        for i, v in enumerate([gap_hbm, gain_hbm, shift_hbm, out_shift_hbm, gate_hbm])
+    ]
+    load_pairs.start()
+    load_first.start()
     load_src.start()
+    for load in load_vecs:
+        load.start()
     load_bias.start()
     load_w.start()
     load_ow.start()
@@ -78,6 +90,7 @@
             barrier, inc=1, device_id={"res": res_peer(t)}, device_id_type=MESH
         )
 
+    load_pairs.wait()
     listed = pairs_ref[...]
     shift_bits = L.bit_length() - 1
     owner = lax.shift_right_arithmetic(listed, jnp.full_like(listed, shift_bits))
@@ -101,6 +114,7 @@
     load_pos = pltpu.make_async_copy(pos_v, pos_s, local_sem.at[4])
     load_pos.start()
 
+    load_first.wait()
     col0 = me_j * cols
     chain_a = jnp.int32(0)
     chain_b = jnp.int32(0)
@@ -133,10 +147,11 @@
             device_id={"res": res_peer(2 * t)}, device_id_type=MESH,
         ).start()
 
-    gap = vec_ref[0:1, :]
-    gain = vec_ref[1:2, :]
-    shift = vec_ref[2:3, :]
-    out_shift = vec_ref[3:4, :]
+    for load in load_vecs:
+        load.wait()
+    gap, gain, shift, out_shift, gate_shift = [
+        v[...].astype(f32).reshape(1, width) for v in vec_refs
+    ]
     load_src.wait()
     step = 4
 
@@ -207,7 +222,7 @@
         wk_t[own, :] = w_h[hd : 2 * hd]
         wqvg_t[1 * width + h * hd : 1 * width + (h + 1) * hd, :] = w_h[2 * hd : 3 * hd]
         wqvg_t[2 * width + h * hd : 2 * width + (h + 1) * hd, :] = w_h[3 * hd :]
-    gate_col[...] = jnp.broadcast_to(vec_ref[4:5, :], (128, width)).T
+    gate_col[...] = jnp.broadcast_to(gate_shift, (128, width)).T
 
     wait_recv(recv_a0.at[pl.ds(0, 2 * (R - 1))], a_recv.at[0])
 
@@ -294,12 +309,12 @@
             ).start()
 
         pltpu.make_async_copy(
-            send_c.at[r * J + me_j], out_hbm.at[me_j * n + r], local_sem.at[6 + r]
+            send_c.at[r * J + me_j], out_hbm.at[me_j * n + r], local_sem.at[13 + r]
         ).start()
 
     for r in range(n):
         pltpu.make_async_copy(
-            send_c.at[r * J + me_j], out_hbm.at[me_j * n + r], local_sem.at[6 + r]
+            send_c.at[r * J + me_j], out_hbm.at[me_j * n + r], local_sem.at[13 + r]
         ).wait()
     wait_send(table_v.at[pl.ds(0, R - 1)], idx_send)
     wait_send(bias_all.at[pl.ds(0, Y - 1), 0], bias_send.at[0])
@@ -332,20 +347,17 @@
     n = L // J
     N = J * cols
     half = width // 2
-    vectors = jnp.stack(
-        [gap_embedding, layer_norm_gain, layer_norm_bias, output_bias, gate_bias_heads]
-    ).astype(f32)
     DMA = pltpu.SemaphoreType.DMA
-    vmem, anywhere = pl.BlockSpec(memory_space=pltpu.VMEM), pl.BlockSpec(memory_space=pl.ANY)
+    hbm = pl.BlockSpec(memory_space=pltpu.HBM)
     return pl.pallas_call(
         functools.partial(body, R, J, n, cols, heads, chains),
         out_shape=jax.ShapeDtypeStruct((L, cols, width), bf16),
-        in_specs=[
-            pl.BlockSpec(memory_space=pltpu.SMEM), vmem, vmem,
-            anywhere, anywhere, anywhere, anywhere,
-        ],
-        out_specs=anywhere,
+        in_specs=[hbm] * 11,
+        out_specs=hbm,
         scratch_shapes=[
+            pltpu.SMEM((chains,), i32),
+            pltpu.VMEM((chains, L), i32),
+            [pltpu.VMEM((width,), bf16)] * 5,
             pltpu.VMEM((L, cols, width), bf16),
             pltpu.VMEM((L, cols, width), bf16),
             pltpu.VMEM((width, heads, 128), bf16),
@@ -372,15 +384,16 @@
             pltpu.VMEM((width, N), bf16),
             pltpu.VMEM((n * J, cols, width), bf16),
             pltpu.VMEM((width, 128), f32),
-            DMA((6 + n,)), DMA, DMA, DMA((2,)), DMA((2,)),
+            DMA((13 + n,)), DMA, DMA, DMA((2,)), DMA((2,)),
             DMA((2,)), DMA((2,)), DMA((2,)), DMA, DMA((n,)), DMA, DMA,
         ],
         compiler_params=pltpu.CompilerParams(
-            collective_id=0, has_side_effects=True, vmem_limit_bytes=40 * 1024 * 1024
+            collective_id=0, has_side_effects=True, vmem_limit_bytes=63 * 1024 * 1024
         ),
     )(
-        chain_first_residue, pairs, vectors, source_alignment_rows, projection_weight,
-        pair_bias_logits, output_weight,
+        chain_first_residue, pairs, gap_embedding, layer_norm_gain,
+        layer_norm_bias, output_bias, gate_bias_heads,
+        source_alignment_rows, projection_weight, pair_bias_logits, output_weight,
     )
 
 

time: 69.8 us -> 63 us (0.903)
  local copies, waits for them, and re-layouts: 7.95 us -> 1.87 us
    unnamed x21 -> x1, local copies, waits for them, and re-layouts: 7.24 us -> 1.87 us
    another operation x6 -> x0, local copies, waits for them, and re-layouts: 0.72 us -> none  [local(): jnp.stack([gap_embedding, layer_norm_gain, layer_norm_bias, output_bias,...]
where the time goes in v2:
time: 63 us; the launch traced here: 62.8 us
  Pallas kernels  60.9 us (97%)
  local copies, waits for them, and re-layouts  1.87 us (3%)
    pallas_call x1, Pallas kernels, local(): pl.pallas_call(functools.partial(body, R, J, n, cols, heads, chains), out...  60.9 us
    unnamed x1, local copies, waits for them, and re-layouts  1.87 us

profile of v2, /device:TPU:1, one launch (start us, length us, event | category | flops | bytes accessed | tf_op | source)
XLA Modules:
  0.0 62.8 jit_solution(4783260218114005972)
XLA Ops:
  0.0 60.9 %shard_map.109 = bf16[64,16,256]{2,1,0:T(8,128)(2,1)} custom-call(s32[6]{0:T(128)} %first_hbm.1, s32[6,64]{1,0:T(8,128)} %pairs_hbm.1, bf16[256]{0:T(256)(128)(2,1)} %gap_hbm.1, bf16[256]{0:T(256)(128)(2,1)} %gain_hbm.1, bf16[256]{0:T(256)(128)(2,1)} %shift_hbm.1, bf16[256]{0:T(256)(128)(2,1)} %out_shift_hbm.1, bf16[256]{0:T(256)(128)(2,1)} %gate_hbm.1, ...), custom_call_target="tpu_custom_call" | custom-call | tf_op jit(solution)/shard_map/pallas_call | solution.py:352
  61.0 1.9 %copy.13 = bf16[64,16,256]{2,1,0:T(8,128)(2,1)} copy(bf16[64,16,256]{2,1,0:T(8,128)(2,1)} %shard_map.109) | data formatting | bytes 1048576

commit v3 on v2

--- a/solution.py
+++ b/solution.py
@@ -34,7 +34,7 @@
     bias_all, bias_t,
     send_a0, send_a1, recv_a0, recv_a1,
     send_b0, send_b1, recv_b0, recv_b1,
-    q_diag, att_v, send_c, gate_col,
+    q_diag, att_v, send_c, gate_col, score_v, lifted_v, v_ext, gate_v,
     local_sem, idx_send, idx_recv, bias_send, bias_recv,
     a_send, a_recv, b_send, b0_recv, b1_recv, c_send, c_recv,
 ):
@@ -49,11 +49,22 @@
     me_j = lax.axis_index("res")
     core = lax.rem(me_j, 2)
 
+    X = 4
+    Z = R // X
+    me_z, me_x = me_r // X, lax.rem(me_r, X)
+
+    def farthest_first(size, i):
+        odd = lax.rem(i, 2)
+        return size // 2 + (1 - 2 * odd) * ((i + odd) // 2)
+
     def row_peer(t):
-        return lax.rem(me_r + t, R)
+        z = lax.rem(me_z + farthest_first(Z, t // X), Z)
+        x = lax.rem(me_x + farthest_first(X, lax.rem(t, X)), X)
+        return z * X + x
 
     def res_peer(t):
-        return lax.rem(me_j + t, J)
+        y = lax.rem(me_j // 2 + farthest_first(Y, t // 2), Y)
+        return 2 * y + lax.rem(core + 1 + lax.rem(t, 2), 2)
 
     load_src = pltpu.make_async_copy(src_hbm, src_v, local_sem.at[0])
     load_w = pltpu.make_async_copy(w_hbm, w_v, local_sem.at[1])
@@ -78,13 +89,13 @@
 
     barrier = pltpu.get_barrier_semaphore()
 
-    @pl.loop(1, R)
+    @pl.loop(0, R - 1)
     def _(t):
         pl.semaphore_signal(
             barrier, inc=1, device_id={"rows": row_peer(t)}, device_id_type=MESH
         )
 
-    @pl.loop(1, J)
+    @pl.loop(0, J - 1)
     def _(t):
         pl.semaphore_signal(
             barrier, inc=1, device_id={"res": res_peer(t)}, device_id_type=MESH
@@ -129,7 +140,7 @@
 
     wanted_v[me_r] = table_v[me_r]
 
-    @pl.loop(1, R)
+    @pl.loop(0, R - 1)
     def _(t):
         b = row_peer(t)
         pltpu.make_async_remote_copy(
@@ -140,11 +151,11 @@
     load_bias.wait()
     my_bias = bias_all.at[me_j // 2, core]
 
-    @pl.loop(1, Y)
+    @pl.loop(0, Y - 1)
     def _(t):
         pltpu.make_async_remote_copy(
             my_bias, my_bias, bias_send.at[0], bias_recv.at[0],
-            device_id={"res": res_peer(2 * t)}, device_id_type=MESH,
+            device_id={"res": res_peer(2 * t + 1)}, device_id_type=MESH,
         ).start()
 
     for load in load_vecs:
@@ -186,7 +197,7 @@
         at_b = jnp.clip(wanted_s[b, 0, k * CHAIN_PAD + chain_b], 0, L - 1)
         return jnp.where(in_b, norm_v[at_b], norm_v[at_a])
 
-    @pl.loop(1, R)
+    @pl.loop(0, R - 1)
     def _(t):
         b = row_peer(t)
         for k in range(2):
@@ -198,7 +209,7 @@
             device_id={"rows": b}, device_id_type=MESH,
         ).start()
 
-    @pl.loop(1, R)
+    @pl.loop(0, R - 1)
     def _(t):
         b = row_peer(t)
         pltpu.make_async_remote_copy(
@@ -215,13 +226,16 @@
     load_ow.wait()
     w_wide[...] = w_v[...].astype(f32).reshape(width * heads, 128)
     q_diag[...] = jnp.zeros_like(q_diag)
-    for h in range(heads):
+    v_ext[...] = jnp.ones_like(v_ext)
+
+    @pl.loop(0, heads)
+    def _(h):
         w_h = w_wide[pl.ds(h, width, stride=heads), :].T.astype(bf16)
-        own = slice(h * hd, (h + 1) * hd)
-        wqvg_t[0 * width + h * hd : 0 * width + (h + 1) * hd, :] = w_h[0:hd]
-        wk_t[own, :] = w_h[hd : 2 * hd]
-        wqvg_t[1 * width + h * hd : 1 * width + (h + 1) * hd, :] = w_h[2 * hd : 3 * hd]
-        wqvg_t[2 * width + h * hd : 2 * width + (h + 1) * hd, :] = w_h[3 * hd :]
+        wqvg_t[0, h] = w_h[0:hd]
+        wk_t[h] = w_h[hd : 2 * hd]
+        wqvg_t[1, h] = w_h[2 * hd : 3 * hd]
+        wqvg_t[2, h] = w_h[3 * hd :]
+
     gate_col[...] = jnp.broadcast_to(gate_shift, (128, width)).T
 
     wait_recv(recv_a0.at[pl.ds(0, 2 * (R - 1))], a_recv.at[0])
@@ -231,7 +245,7 @@
         at_b = jnp.clip(pos_s[chain_b, s], 0, 2 * R)
         return jnp.where(in_b_half, recv[at_b], recv[at_a])
 
-    @pl.loop(1, J)
+    @pl.loop(0, J - 1)
     def _(t):
         j = res_peer(t)
         for r in range(n):
@@ -255,7 +269,7 @@
 
     @pl.loop(0, n)
     def _(r):
-        @pl.loop(1, J)
+        @pl.loop(0, J - 1)
         def _(t):
             j = res_peer(t)
             send_b1[r, j] = regather(recv_a1, j * n + r)
@@ -267,7 +281,9 @@
         recv_b1[r, me_j] = regather(recv_a1, me_j * n + r)
 
     wait_recv(bias_all.at[:, 0], bias_recv.at[1])
-    for h in range(heads):
+
+    @pl.loop(0, heads)
+    def _(h):
         block = bias_all[:, :, h].reshape(N, N).astype(f32)
         bias_t[h] = block.T * log2e
 
@@ -280,27 +296,37 @@
         x = jnp.concatenate(
             [recv_b0[r].reshape(N, half), recv_b1[r].reshape(N, half)], axis=1
         )
-        qvg = lax.dot_general(wqvg_t[...], x, NT, preferred_element_type=f32)
-        keys = lax.dot_general(x, wk_t[...], NT, preferred_element_type=f32).astype(bf16)
+        qvg = lax.dot_general(
+            wqvg_t[...].reshape(3 * width, width), x, NT, preferred_element_type=f32
+        )
+        keys = lax.dot_general(
+            x, wk_t[...].reshape(width, width), NT, preferred_element_type=f32
+        ).astype(bf16)
         q = (qvg[:width] * scale).astype(bf16)
         v = qvg[width : 2 * width].astype(bf16)
-        gate = jax.nn.sigmoid(qvg[2 * width :] + gate_col[:, 0:1])
-        ones = jnp.ones((16, N), bf16)
+        gate_v[...] = jax.nn.sigmoid(qvg[2 * width :] + gate_col[:, 0:1])
         for h in range(heads):
             own = slice(h * hd, (h + 1) * hd)
-            q_diag[h, own, :] = q[own]
-            s = jnp.dot(keys, q_diag[h], preferred_element_type=f32) + bias_t[h]
+            q_diag[own, h * N : (h + 1) * N] = q[own]
+            v_ext[h, :hd, :] = v[own]
+        score_v[...] = jnp.dot(keys, q_diag[...], preferred_element_type=f32)
+        part = min(N, 128)
+        for t in range(heads * N // part):
+            h, at = t * part // N, t * part % N
+            s = score_v[:, t * part : (t + 1) * part] + bias_t[h, :, at : at + part]
             top = jnp.max(s, axis=0, keepdims=True)
-            e = jnp.exp2(s - top).astype(bf16)
+            lifted_v[:, t * part : (t + 1) * part] = jnp.exp2(s - top).astype(bf16)
+        for h in range(heads):
+            own = slice(h * hd, (h + 1) * hd)
             o = jnp.dot(
-                jnp.concatenate([v[own], ones], axis=0), e, preferred_element_type=f32
+                v_ext[h], lifted_v[:, h * N : (h + 1) * N], preferred_element_type=f32
             )
-            att_v[own, :] = (o[:hd] * (1.0 / o[hd : hd + 1]) * gate[own]).astype(bf16)
+            att_v[own, :] = (o[:hd] * (1.0 / o[hd : hd + 1]) * gate_v[own]).astype(bf16)
         update = lax.dot_general(att_v[...], ow_v[...], TN, preferred_element_type=f32)
         update = (update + out_shift).astype(bf16)
         send_c[pl.ds(r * J, J)] = update.reshape(J, cols, width)
 
-        @pl.loop(1, J)
+        @pl.loop(0, J - 1)
         def _(t):
             j = res_peer(t)
             pltpu.make_async_remote_copy(
@@ -362,8 +388,8 @@
             pltpu.VMEM((L, cols, width), bf16),
             pltpu.VMEM((width, heads, 128), bf16),
             pltpu.VMEM((width * heads, 128), f32),
-            pltpu.VMEM((3 * width, width), bf16),
-            pltpu.VMEM((width, width), bf16),
+            pltpu.VMEM((3, heads, width // heads, width), bf16),
+            pltpu.VMEM((heads, width // heads, width), bf16),
             pltpu.VMEM((width, width), bf16),
             pltpu.VMEM((R, 1, 128), i32),
             pltpu.VMEM((R, 1, 128), i32),
@@ -380,10 +406,14 @@
             pltpu.VMEM((n, J, cols, half), bf16),
             pltpu.VMEM((n, J, cols, half), bf16),
             pltpu.VMEM((n, J, cols, half), bf16),
-            pltpu.VMEM((heads, width, N), bf16),
+            pltpu.VMEM((width, heads * N), bf16),
             pltpu.VMEM((width, N), bf16),
             pltpu.VMEM((n * J, cols, width), bf16),
             pltpu.VMEM((width, 128), f32),
+            pltpu.VMEM((N, heads * N), f32),
+            pltpu.VMEM((N, heads * N), bf16),
+            pltpu.VMEM((heads, width // heads + 16, N), bf16),
+            pltpu.VMEM((width, N), f32),
             DMA((13 + n,)), DMA, DMA, DMA((2,)), DMA((2,)),
             DMA((2,)), DMA((2,)), DMA((2,)), DMA, DMA((n,)), DMA, DMA,
         ],

time: 63 us -> 59.5 us (0.944)
  Pallas kernels: 60.9 us -> 57.5 us
    pallas_call x1, Pallas kernels: 60.9 us -> 57.5 us  [local(): pl.pallas_call(functools.partial(body, R, J, n, cols, heads, chains), out...]
where the time goes in v3:
time: 59.5 us; the launch traced here: 59.4 us
  Pallas kernels  57.5 us (97%)
  local copies, waits for them, and re-layouts  1.87 us (3%)
    pallas_call x1, Pallas kernels, local(): pl.pallas_call(functools.partial(body, R, J, n, cols, heads, chains), out...  57.5 us
    unnamed x1, local copies, waits for them, and re-layouts  1.87 us

profile of v3, /device:TPU:1, one launch (start us, length us, event | category | flops | bytes accessed | tf_op | source)
XLA Modules:
  0.0 59.4 jit_solution(7329522244316814428)
XLA Ops:
  0.0 57.5 %shard_map.109 = bf16[64,16,256]{2,1,0:T(8,128)(2,1)} custom-call(s32[6]{0:T(128)} %first_hbm.1, s32[6,64]{1,0:T(8,128)} %pairs_hbm.1, bf16[256]{0:T(256)(128)(2,1)} %gap_hbm.1, bf16[256]{0:T(256)(128)(2,1)} %gain_hbm.1, bf16[256]{0:T(256)(128)(2,1)} %shift_hbm.1, bf16[256]{0:T(256)(128)(2,1)} %out_shift_hbm.1, bf16[256]{0:T(256)(128)(2,1)} %gate_hbm.1, ...), custom_call_target="tpu_custom_call" | custom-call | tf_op jit(solution)/shard_map/pallas_call | solution.py:378
  57.5 1.9 %copy.13 = bf16[64,16,256]{2,1,0:T(8,128)(2,1)} copy(bf16[64,16,256]{2,1,0:T(8,128)(2,1)} %shard_map.109) | data formatting | bytes 1048576

commit v4 on v3

--- a/solution.py
+++ b/solution.py
@@ -34,7 +34,7 @@
     bias_all, bias_t,
     send_a0, send_a1, recv_a0, recv_a1,
     send_b0, send_b1, recv_b0, recv_b1,
-    q_diag, att_v, send_c, gate_col, score_v, lifted_v, v_ext, gate_v,
+    q_diag, att_v, send_c, gate_col, lifted_v, v_ext, gate_v,
     local_sem, idx_send, idx_recv, bias_send, bias_recv,
     a_send, a_recv, b_send, b0_recv, b1_recv, c_send, c_recv,
 ):
@@ -58,13 +58,13 @@
         return size // 2 + (1 - 2 * odd) * ((i + odd) // 2)
 
     def row_peer(t):
-        z = lax.rem(me_z + farthest_first(Z, t // X), Z)
-        x = lax.rem(me_x + farthest_first(X, lax.rem(t, X)), X)
+        z = lax.rem(me_z + farthest_first(Z, lax.rem(t, Z)), Z)
+        x = lax.rem(me_x + farthest_first(X, t // Z), X)
         return z * X + x
 
     def res_peer(t):
-        y = lax.rem(me_j // 2 + farthest_first(Y, t // 2), Y)
-        return 2 * y + lax.rem(core + 1 + lax.rem(t, 2), 2)
+        y = lax.rem(me_j // 2 + farthest_first(Y, lax.rem(t, Y)), Y)
+        return 2 * y + lax.rem(core + 1 + t // Y, 2)
 
     load_src = pltpu.make_async_copy(src_hbm, src_v, local_sem.at[0])
     load_w = pltpu.make_async_copy(w_hbm, w_v, local_sem.at[1])
@@ -155,7 +155,7 @@
     def _(t):
         pltpu.make_async_remote_copy(
             my_bias, my_bias, bias_send.at[0], bias_recv.at[0],
-            device_id={"res": res_peer(2 * t + 1)}, device_id_type=MESH,
+            device_id={"res": res_peer(Y + t)}, device_id_type=MESH,
         ).start()
 
     for load in load_vecs:
@@ -164,7 +164,7 @@
         v[...].astype(f32).reshape(1, width) for v in vec_refs
     ]
     load_src.wait()
-    step = 4
+    step = min(16, L)
 
     @pl.loop(0, L // step)
     def _(i):
@@ -265,11 +265,18 @@
         device_id={"res": me_j + 1 - 2 * core}, device_id_type=MESH,
     ).start()
 
+    wait_recv(bias_all.at[:, 0], bias_recv.at[1])
+
+    @pl.loop(0, heads)
+    def _(h):
+        block = bias_all[:, :, h].reshape(N, N).astype(f32)
+        bias_t[h] = block.T * log2e
+
     wait_recv(recv_a1.at[pl.ds(0, 2 * (R - 1))], a_recv.at[1])
 
     @pl.loop(0, n)
     def _(r):
-        @pl.loop(0, J - 1)
+        @pl.loop(0, J - 1, unroll=5)
         def _(t):
             j = res_peer(t)
             send_b1[r, j] = regather(recv_a1, j * n + r)
@@ -279,13 +286,6 @@
             ).start()
 
         recv_b1[r, me_j] = regather(recv_a1, me_j * n + r)
-
-    wait_recv(bias_all.at[:, 0], bias_recv.at[1])
-
-    @pl.loop(0, heads)
-    def _(h):
-        block = bias_all[:, :, h].reshape(N, N).astype(f32)
-        bias_t[h] = block.T * log2e
 
     wait_recv(recv_b0.at[:, pl.ds(0, J - 1)], b0_recv)
     scale = hd ** (-0.5) * log2e
@@ -309,13 +309,11 @@
             own = slice(h * hd, (h + 1) * hd)
             q_diag[own, h * N : (h + 1) * N] = q[own]
             v_ext[h, :hd, :] = v[own]
-        score_v[...] = jnp.dot(keys, q_diag[...], preferred_element_type=f32)
-        part = min(N, 128)
-        for t in range(heads * N // part):
-            h, at = t * part // N, t * part % N
-            s = score_v[:, t * part : (t + 1) * part] + bias_t[h, :, at : at + part]
+        for h in range(heads):
+            at = slice(h * N, (h + 1) * N)
+            s = jnp.dot(keys, q_diag[:, at], preferred_element_type=f32) + bias_t[h]
             top = jnp.max(s, axis=0, keepdims=True)
-            lifted_v[:, t * part : (t + 1) * part] = jnp.exp2(s - top).astype(bf16)
+            lifted_v[:, at] = jnp.exp2(s - top).astype(bf16)
         for h in range(heads):
             own = slice(h * hd, (h + 1) * hd)
             o = jnp.dot(
@@ -410,7 +408,6 @@
             pltpu.VMEM((width, N), bf16),
             pltpu.VMEM((n * J, cols, width), bf16),
             pltpu.VMEM((width, 128), f32),
-            pltpu.VMEM((N, heads * N), f32),
             pltpu.VMEM((N, heads * N), bf16),
             pltpu.VMEM((heads, width // heads + 16, N), bf16),
             pltpu.VMEM((width, N), f32),

time: 59.5 us -> 59.1 us (level)
  no operation moved by 1% of the time
where the time goes in v4:
time: 59.1 us; the launch traced here: 58.9 us
  Pallas kernels  57.1 us (97%)
  local copies, waits for them, and re-layouts  1.87 us (3%)
    pallas_call x1, Pallas kernels, local(): pl.pallas_call(functools.partial(body, R, J, n, cols, heads, chains), out...  57.1 us
    unnamed x1, local copies, waits for them, and re-layouts  1.87 us

profile of v4, /device:TPU:1, one launch (start us, length us, event | category | flops | bytes accessed | tf_op | source)
XLA Modules:
  0.0 58.9 jit_solution(5789773083373647194)
XLA Ops:
  0.0 57.1 %shard_map.109 = bf16[64,16,256]{2,1,0:T(8,128)(2,1)} custom-call(s32[6]{0:T(128)} %first_hbm.1, s32[6,64]{1,0:T(8,128)} %pairs_hbm.1, bf16[256]{0:T(256)(128)(2,1)} %gap_hbm.1, bf16[256]{0:T(256)(128)(2,1)} %gain_hbm.1, bf16[256]{0:T(256)(128)(2,1)} %shift_hbm.1, bf16[256]{0:T(256)(128)(2,1)} %out_shift_hbm.1, bf16[256]{0:T(256)(128)(2,1)} %gate_hbm.1, ...), custom_call_target="tpu_custom_call" | custom-call | tf_op jit(solution)/shard_map/pallas_call | solution.py:376
  57.1 1.9 %copy.13 = bf16[64,16,256]{2,1,0:T(8,128)(2,1)} copy(bf16[64,16,256]{2,1,0:T(8,128)(2,1)} %shard_map.109) | data formatting | bytes 1048576

commit v5 on v4

--- a/solution.py
+++ b/solution.py
@@ -164,7 +164,7 @@
         v[...].astype(f32).reshape(1, width) for v in vec_refs
     ]
     load_src.wait()
-    step = min(16, L)
+    step = min(8, L)
 
     @pl.loop(0, L // step)
     def _(i):
@@ -276,7 +276,7 @@
 
     @pl.loop(0, n)
     def _(r):
-        @pl.loop(0, J - 1, unroll=5)
+        @pl.loop(0, J - 1)
         def _(t):
             j = res_peer(t)
             send_b1[r, j] = regather(recv_a1, j * n + r)

time: 59.1 us -> 58.6 us (level)
  no operation moved by 1% of the time
where the time goes in v5:
time: 58.6 us; the launch traced here: 58.5 us
  Pallas kernels  56.6 us (97%)
  local copies, waits for them, and re-layouts  1.87 us (3%)
    pallas_call x1, Pallas kernels, local(): pl.pallas_call(functools.partial(body, R, J, n, cols, heads, chains), out...  56.6 us
    unnamed x1, local copies, waits for them, and re-layouts  1.87 us

profile of v5, /device:TPU:1, one launch (start us, length us, event | category | flops | bytes accessed | tf_op | source)
XLA Modules:
  0.0 58.5 jit_solution(3202176587201470354)
XLA Ops:
  0.0 56.6 %shard_map.109 = bf16[64,16,256]{2,1,0:T(8,128)(2,1)} custom-call(s32[6]{0:T(128)} %first_hbm.1, s32[6,64]{1,0:T(8,128)} %pairs_hbm.1, bf16[256]{0:T(256)(128)(2,1)} %gap_hbm.1, bf16[256]{0:T(256)(128)(2,1)} %gain_hbm.1, bf16[256]{0:T(256)(128)(2,1)} %shift_hbm.1, bf16[256]{0:T(256)(128)(2,1)} %out_shift_hbm.1, bf16[256]{0:T(256)(128)(2,1)} %gate_hbm.1, ...), custom_call_target="tpu_custom_call" | custom-call | tf_op jit(solution)/shard_map/pallas_call | solution.py:376
  56.6 1.9 %copy.13 = bf16[64,16,256]{2,1,0:T(8,128)(2,1)} copy(bf16[64,16,256]{2,1,0:T(8,128)(2,1)} %shard_map.109) | data formatting | bytes 1048576

commit v6 on v5

--- a/solution.py
+++ b/solution.py
@@ -1,5 +1,4 @@
 import functools
-import math
 
 import jax
 import jax.numpy as jnp
@@ -44,7 +43,6 @@
     N = J * cols
     hd = width // heads
     Y = J // 2
-    log2e = math.log2(math.e)
     me_r = lax.axis_index("rows")
     me_j = lax.axis_index("res")
     core = lax.rem(me_j, 2)
@@ -270,7 +268,7 @@
     @pl.loop(0, heads)
     def _(h):
         block = bias_all[:, :, h].reshape(N, N).astype(f32)
-        bias_t[h] = block.T * log2e
+        bias_t[h] = block.T
 
     wait_recv(recv_a1.at[pl.ds(0, 2 * (R - 1))], a_recv.at[1])
 
@@ -288,7 +286,7 @@
         recv_b1[r, me_j] = regather(recv_a1, me_j * n + r)
 
     wait_recv(recv_b0.at[:, pl.ds(0, J - 1)], b0_recv)
-    scale = hd ** (-0.5) * log2e
+    scale = hd ** (-0.5)
 
     @pl.loop(0, n)
     def _(r):
@@ -313,7 +311,7 @@
             at = slice(h * N, (h + 1) * N)
             s = jnp.dot(keys, q_diag[:, at], preferred_element_type=f32) + bias_t[h]
             top = jnp.max(s, axis=0, keepdims=True)
-            lifted_v[:, at] = jnp.exp2(s - top).astype(bf16)
+            lifted_v[:, at] = jnp.exp(s - top).astype(bf16)
         for h in range(heads):
             own = slice(h * hd, (h + 1) * hd)
             o = jnp.dot(

time: 58.6 us -> 58.8 us (level)
  no operation moved by 1% of the time
where the time goes in v6:
time: 58.8 us; the launch traced here: 58.6 us
  Pallas kernels  56.7 us (96%)
  local copies, waits for them, and re-layouts  1.87 us (3%)
    pallas_call x1, Pallas kernels, local(): pl.pallas_call(functools.partial(body, R, J, n, cols, heads, chains), out...  56.7 us
    unnamed x1, local copies, waits for them, and re-layouts  1.87 us

profile of v6, /device:TPU:1, one launch (start us, length us, event | category | flops | bytes accessed | tf_op | source)
XLA Modules:
  0.0 58.6 jit_solution(15418178933024609438)
XLA Ops:
  0.0 56.7 %shard_map.109 = bf16[64,16,256]{2,1,0:T(8,128)(2,1)} custom-call(s32[6]{0:T(128)} %first_hbm.1, s32[6,64]{1,0:T(8,128)} %pairs_hbm.1, bf16[256]{0:T(256)(128)(2,1)} %gap_hbm.1, bf16[256]{0:T(256)(128)(2,1)} %gain_hbm.1, bf16[256]{0:T(256)(128)(2,1)} %shift_hbm.1, bf16[256]{0:T(256)(128)(2,1)} %out_shift_hbm.1, bf16[256]{0:T(256)(128)(2,1)} %gate_hbm.1, ...), custom_call_target="tpu_custom_call" | custom-call | tf_op jit(solution)/shard_map/pallas_call | solution.py:374
  56.7 1.9 %copy.13 = bf16[64,16,256]{2,1,0:T(8,128)(2,1)} copy(bf16[64,16,256]{2,1,0:T(8,128)(2,1)} %shard_map.109) | data formatting | bytes 1048576
